TPU v7x, 32 devices: a whole 2x2x4 slice. The times are simulated.
32 devices in a mesh: dp: 4 (over y, core), mp: 8 (over z, x).
Axes of the slice: x: 2, y: 2, z: 4, core: 2. Of those that a mesh axis runs over, the one named last changes fastest.
Arguments:
- patches: bfloat16 [8, 24, 24, 1024], P('dp', None, None, 'mp'), may hold values from -6 to 6
- first_reduce: bfloat16 [1024, 1024], P(None, 'mp'), may hold values from -0.1875 to 0.1875
- first_mixer: bfloat16 [3, 3, 1024, 1024], P(None, None, 'mp'), may hold values from -0.0625 to 0.0625
- first_expand: bfloat16 [1024, 1024], P('mp'), may hold values from -0.1875 to 0.1875
- first_gain: float32 [1024], P('mp'), may hold values from 0.1 to 1.9
- first_shift: float32 [1024], P('mp'), may hold values from -3 to 3
- second_reduce: bfloat16 [1024, 1024], P(None, 'mp'), may hold values from -0.1875 to 0.1875
- second_mixer: bfloat16 [3, 3, 1024, 1024], P(None, None, 'mp'), may hold values from -0.0625 to 0.0625
- second_expand: bfloat16 [1024, 1024], P('mp'), may hold values from -0.1875 to 0.1875
- second_gain: float32 [1024], P('mp'), may hold values from 0.1 to 1.9
- second_shift: float32 [1024], P('mp'), may hold values from -3 to 3
- readout_in: bfloat16 [1024, 4096], P(None, 'mp'), may hold values from -0.1875 to 0.1875
- readout_out: bfloat16 [4096, 4096], P('mp'), may hold values from -0.09375 to 0.09375
- cotangent: bfloat16 [1152, 4096], P('dp', 'mp'), may hold values from -6 to 6
- live_counts: int32 [4], P('dp'), may hold values from 1 to 2, as said below
Outputs:
- tokens: bfloat16 [1152, 4096], P('dp', 'mp')
- patch_grads: float32 [8, 24, 24, 1024], P('dp', None, None, 'mp')
- first_reduce_grad: float32 [1024, 1024], P(None, 'mp')
- first_mixer_grad: float32 [3, 3, 1024, 1024], P(None, None, 'mp')
- first_expand_grad: float32 [1024, 1024], P('mp')
- first_gain_grad: float32 [1024], P('mp')
- first_shift_grad: float32 [1024], P('mp')
- second_reduce_grad: float32 [1024, 1024], P(None, 'mp')
- second_mixer_grad: float32 [3, 3, 1024, 1024], P(None, None, 'mp')
- second_expand_grad: float32 [1024, 1024], P('mp')
- second_gain_grad: float32 [1024], P('mp')
- second_shift_grad: float32 [1024], P('mp')
- readout_in_grad: float32 [1024, 4096], P(None, 'mp')
- readout_out_grad: float32 [4096, 4096], P('mp')
Inputs may be any that keep to these rules, and one draw needn't show every extreme that they name: `live_counts`: live grid slots of each data group; 2 in at least one group.
All inputs are finite; a program needn't handle non-finite values.
Results may differ from a plain program's by a relative error of at most 0.03.
Values may be sent and summed in bfloat16 or wider, within the bound.
A program may use at most 128 MiB of HBM per device.

v0:
```python
import jax
import jax.numpy as jnp
from jax import lax
from jax.sharding import PartitionSpec as P

norm_eps = 1e-06


def conv_same(image, kernel):
    return lax.conv_general_dilated(
        image,
        kernel,
        (1, 1),
        "SAME",
        dimension_numbers=("NHWC", "HWIO", "NHWC"),
        preferred_element_type=jnp.float32,
    )


def silu_back(values, grad_values):
    return jax.vjp(jax.nn.silu, values)[1](grad_values)[0]


def gelu_exact(values):
    return jax.nn.gelu(values, approximate=False)


def gelu_back(values, grad_values):
    return jax.vjp(gelu_exact, values)[1](grad_values)[0]


def block_forward(inputs, reduce_w, mixer_w, expand_w, gain, shift):
    num_grids, grid_height, grid_width, local_chans = inputs.shape
    pixel_rows = num_grids * grid_height * grid_width
    low_in = inputs.astype(jnp.bfloat16).reshape(pixel_rows, local_chans)
    full_in = lax.all_gather(low_in, "mp", axis=1, tiled=True)
    total_chans = full_in.shape[1]
    pre_act = jnp.dot(full_in, reduce_w, preferred_element_type=jnp.float32)
    hidden = jax.nn.silu(pre_act).astype(jnp.bfloat16)
    partial_mix = conv_same(
        hidden.reshape(num_grids, grid_height, grid_width, local_chans), mixer_w
    )
    mixed_sum = lax.psum_scatter(
        partial_mix.reshape(pixel_rows, total_chans).astype(jnp.bfloat16),
        "mp",
        scatter_dimension=1,
        tiled=True,
    ).astype(jnp.float32)
    row_total, row_squares = lax.psum(
        (jnp.sum(mixed_sum, axis=1), jnp.sum(mixed_sum * mixed_sum, axis=1)), "mp"
    )
    center = row_total / total_chans
    inv_std = lax.rsqrt(row_squares / total_chans - center * center + norm_eps)
    normed = (mixed_sum - center[:, None]) * inv_std[:, None]
    affine = normed * gain + shift
    branch_in = jax.nn.silu(affine).astype(jnp.bfloat16)
    partial_out = jnp.dot(branch_in, expand_w, preferred_element_type=jnp.float32)
    branch_out = lax.psum_scatter(
        partial_out.astype(jnp.bfloat16), "mp", scatter_dimension=1, tiled=True
    ).astype(jnp.float32)
    outputs = inputs + branch_out.reshape(inputs.shape)
    return (outputs, (full_in, pre_act, hidden, normed, inv_std, affine, branch_in))


def block_backward(grad_out, saved, reduce_w, mixer_w, expand_w, gain):
    full_in, pre_act, hidden, normed, inv_std, affine, branch_in = saved
    num_grids, grid_height, grid_width, local_chans = grad_out.shape
    pixel_rows = num_grids * grid_height * grid_width
    grad_rows = grad_out.reshape(pixel_rows, local_chans)
    grad_branch = lax.all_gather(grad_rows.astype(jnp.bfloat16), "mp", axis=1, tiled=True)
    total_chans = grad_branch.shape[1]
    expand_grad = jnp.einsum(
        "ri,ro->io", branch_in, grad_branch, preferred_element_type=jnp.float32
    )
    grad_act = jnp.einsum("ro,io->ri", grad_branch, expand_w, preferred_element_type=jnp.float32)
    grad_affine = silu_back(affine, grad_act)
    gain_grad = jnp.sum(grad_affine * normed, axis=0)
    shift_grad = jnp.sum(grad_affine, axis=0)
    scaled = grad_affine * gain
    sum_plain, sum_normed = lax.psum(
        (jnp.sum(scaled, axis=1), jnp.sum(scaled * normed, axis=1)), "mp"
    )
    grad_mixed = inv_std[:, None] * (
        scaled - sum_plain[:, None] / total_chans - normed * sum_normed[:, None] / total_chans
    )
    mixed_full = lax.all_gather(grad_mixed.astype(jnp.bfloat16), "mp", axis=1, tiled=True)
    mixed_image = mixed_full.reshape(num_grids, grid_height, grid_width, total_chans)
    flipped = jnp.transpose(mixer_w[::-1, ::-1], (0, 1, 3, 2))
    grad_hidden = conv_same(mixed_image, flipped).reshape(pixel_rows, local_chans)
    padded = jnp.pad(
        hidden.reshape(num_grids, grid_height, grid_width, local_chans),
        ((0, 0), (1, 1), (1, 1), (0, 0)),
    )
    mixer_grad = jnp.stack(
        [
            jnp.stack(
                [
                    jnp.einsum(
                        "nhwi,nhwo->io",
                        padded[
                            :,
                            offset_h : offset_h + grid_height,
                            offset_w : offset_w + grid_width,
                            :,
                        ],
                        mixed_image,
                        preferred_element_type=jnp.float32,
                    )
                    for offset_w in range(3)
                ]
            )
            for offset_h in range(3)
        ]
    )
    grad_pre = silu_back(pre_act, grad_hidden).astype(jnp.bfloat16)
    reduce_grad = jnp.einsum("ri,ro->io", full_in, grad_pre, preferred_element_type=jnp.float32)
    partial_in = jnp.einsum("ro,io->ri", grad_pre, reduce_w, preferred_element_type=jnp.float32)
    grad_in = (
        lax.psum_scatter(
            partial_in.astype(jnp.bfloat16), "mp", scatter_dimension=1, tiled=True
        ).astype(jnp.float32)
        + grad_rows
    )
    return (
        grad_in.reshape(grad_out.shape),
        (reduce_grad, mixer_grad, expand_grad, gain_grad, shift_grad),
    )


def body(
    patches,
    first_reduce,
    first_mixer,
    first_expand,
    first_gain,
    first_shift,
    second_reduce,
    second_mixer,
    second_expand,
    second_gain,
    second_shift,
    readout_in,
    readout_out,
    cotangent,
    live_counts,
):
    num_grids, grid_height, grid_width, local_chans = patches.shape
    pooled_side = grid_height // 2
    patch_values = patches.astype(jnp.float32)
    first_out = block_forward(
        patch_values, first_reduce, first_mixer, first_expand, first_gain, first_shift
    )[0]
    pooled = first_out.reshape(num_grids, pooled_side, 2, pooled_side, 2, local_chans).mean(
        axis=(2, 4)
    )
    second_out = block_forward(
        pooled, second_reduce, second_mixer, second_expand, second_gain, second_shift
    )[0]
    token_count = num_grids * pooled_side * pooled_side
    flat = second_out.astype(jnp.bfloat16).reshape(token_count, local_chans)
    flat_full = lax.all_gather(flat, "mp", axis=1, tiled=True)
    lifted = jnp.dot(flat_full, readout_in, preferred_element_type=jnp.float32)
    activated = gelu_exact(lifted).astype(jnp.bfloat16)
    partial_tokens = jnp.dot(activated, readout_out, preferred_element_type=jnp.float32)
    summed = lax.psum_scatter(
        partial_tokens.astype(jnp.bfloat16), "mp", scatter_dimension=1, tiled=True
    ).astype(jnp.float32)
    live_slots = (jnp.arange(num_grids) < live_counts[0]).astype(jnp.float32)
    live_rows = jnp.repeat(live_slots, pooled_side * pooled_side)
    tokens = (summed * live_rows[:, None]).astype(jnp.bfloat16)
    grad_tokens = cotangent * live_rows[:, None].astype(jnp.bfloat16)
    grad_full = lax.all_gather(grad_tokens, "mp", axis=1, tiled=True)
    readout_out_grad = jnp.einsum(
        "ri,ro->io", activated, grad_full, preferred_element_type=jnp.float32
    )
    grad_act = jnp.einsum("ro,io->ri", grad_full, readout_out, preferred_element_type=jnp.float32)
    grad_lift = gelu_back(lifted, grad_act).astype(jnp.bfloat16)
    readout_in_grad = jnp.einsum(
        "ri,ro->io", flat_full, grad_lift, preferred_element_type=jnp.float32
    )
    partial_flat = jnp.einsum(
        "ro,io->ri", grad_lift, readout_in, preferred_element_type=jnp.float32
    )
    grad_flat = lax.psum_scatter(
        partial_flat.astype(jnp.bfloat16), "mp", scatter_dimension=1, tiled=True
    ).astype(jnp.float32)
    second_saved = block_forward(
        pooled, second_reduce, second_mixer, second_expand, second_gain, second_shift
    )[1]
    grad_pooled, second_grads = block_backward(
        grad_flat.reshape(num_grids, pooled_side, pooled_side, local_chans),
        second_saved,
        second_reduce,
        second_mixer,
        second_expand,
        second_gain,
    )
    spread_back = jnp.broadcast_to(
        0.25 * grad_pooled[:, :, None, :, None, :],
        (num_grids, pooled_side, 2, pooled_side, 2, local_chans),
    ).reshape(patches.shape)
    first_saved = block_forward(
        patch_values, first_reduce, first_mixer, first_expand, first_gain, first_shift
    )[1]
    patch_grads, first_grads = block_backward(
        spread_back, first_saved, first_reduce, first_mixer, first_expand, first_gain
    )
    summed_grads = (
        lax.psum(first_grads[0].astype(jnp.bfloat16), "dp").astype(jnp.float32),
        lax.psum(first_grads[1].astype(jnp.bfloat16), "dp").astype(jnp.float32),
        lax.psum(first_grads[2].astype(jnp.bfloat16), "dp").astype(jnp.float32),
        lax.psum(first_grads[3].astype(jnp.bfloat16), "dp").astype(jnp.float32),
        lax.psum(first_grads[4].astype(jnp.bfloat16), "dp").astype(jnp.float32),
        lax.psum(second_grads[0].astype(jnp.bfloat16), "dp").astype(jnp.float32),
        lax.psum(second_grads[1].astype(jnp.bfloat16), "dp").astype(jnp.float32),
        lax.psum(second_grads[2].astype(jnp.bfloat16), "dp").astype(jnp.float32),
        lax.psum(second_grads[3].astype(jnp.bfloat16), "dp").astype(jnp.float32),
        lax.psum(second_grads[4].astype(jnp.bfloat16), "dp").astype(jnp.float32),
        lax.psum(readout_in_grad.astype(jnp.bfloat16), "dp").astype(jnp.float32),
        lax.psum(readout_out_grad.astype(jnp.bfloat16), "dp").astype(jnp.float32),
    )
    return (
        tokens,
        patch_grads,
        summed_grads[0],
        summed_grads[1],
        summed_grads[2],
        summed_grads[3],
        summed_grads[4],
        summed_grads[5],
        summed_grads[6],
        summed_grads[7],
        summed_grads[8],
        summed_grads[9],
        summed_grads[10],
        summed_grads[11],
    )


def solution(mesh):
    in_specs = (
        P("dp", None, None, "mp"),
        P(None, "mp"),
        P(None, None, "mp", None),
        P("mp", None),
        P("mp"),
        P("mp"),
        P(None, "mp"),
        P(None, None, "mp", None),
        P("mp", None),
        P("mp"),
        P("mp"),
        P(None, "mp"),
        P("mp", None),
        P("dp", "mp"),
        P("dp"),
    )
    out_specs = (
        P("dp", "mp"),
        P("dp", None, None, "mp"),
        P(None, "mp"),
        P(None, None, "mp", None),
        P("mp", None),
        P("mp"),
        P("mp"),
        P(None, "mp"),
        P(None, None, "mp", None),
        P("mp", None),
        P("mp"),
        P("mp"),
        P(None, "mp"),
        P("mp", None),
    )
    return jax.shard_map(body, mesh=mesh, in_specs=in_specs, out_specs=out_specs, check_vma=False)
```

profile of v0, /device:TPU:0, one launch (start us, length us, event | category | flops | bytes accessed | tf_op | source)
XLA Modules:
  0.0 1254.6 jit_solution(4709107433824589815)
XLA Ops:
  8.0 58.6 %all-gather.5.cloned.1.call-done = bf16[1152,1024]{1,0:T(8,128)(2,1)} async-done(((bf16[1152,128]{1,0:T(8,128)(2,1)}), bf16[1152,1024]{1,0:T(8,128)(2,1)}) %all-gather.5.cloned.1.call-update) | async-done | bytes 2359312 | tf_op jit(solution)/shard_map/all_gather | solution.py:36
  84.1 67.4 %reduce-scatter.25.cloned.1.call-done = bf16[128,1152]{1,0:T(8,128)(2,1)} async-done(((bf16[1024,1152]{1,0:T(8,128)(2,1)}), bf16[128,1152]{1,0:T(8,128)(2,1)}) %reduce-scatter.25.cloned.1.call-update) | async-done | bytes 294928
  153.0 34.9 %all-reduce.5 = (f32[1152]{0:T(1024)S(1)}, f32[1152]{0:T(1024)S(1)}) all-reduce(f32[1152]{0:T(1024)S(1)} %get-tuple-element.75, f32[1152]{0:T(1024)S(1)} %get-tuple-element.74), channel_id=1, replica_groups=mesh['dp'=4,'mp'=8] {'mp'}, use_global_device_ids=true, to_apply=%region_4.5 | all-reduce | flops 2304 | bytes 18432 | tf_op jit(solution)/shard_map/psum | solution.py:49
  194.5 66.4 %reduce-scatter.27.cloned.1.call-done = bf16[128,1152]{1,0:T(8,128)(2,1)} async-done(((bf16[1024,1152]{1,0:T(8,128)(2,1)}), bf16[128,1152]{1,0:T(8,128)(2,1)}) %reduce-scatter.27.cloned.1.call-update) | async-done | bytes 294928
  264.3 28.4 %all_gather.27 = bf16[288,1024]{1,0:T(8,128)(2,1)S(1)} all-gather(bf16[288,128]{1,0:T(8,128)(2,1)S(1)} %convert_element_type.204), channel_id=1, replica_groups=mesh['dp'=4,'mp'=8] {'mp'}, dimensions={1}, use_global_device_ids=true | all-gather | bytes 663552 | tf_op jit(solution)/shard_map/all_gather | solution.py:36
  302.5 59.8 %reduce-scatter.29.cloned.1.call-done = bf16[128,288]{1,0:T(8,128)(2,1)} async-done(((bf16[1024,288]{1,0:T(8,128)(2,1)}), bf16[128,288]{1,0:T(8,128)(2,1)}) %reduce-scatter.29.cloned.1.call-update) | async-done | bytes 73744
  363.5 19.3 %all-reduce.4 = (f32[288]{0:T(512)S(1)}, f32[288]{0:T(512)S(1)}) all-reduce(f32[288]{0:T(512)S(1)} %get-tuple-element.81, f32[288]{0:T(512)S(1)} %get-tuple-element.80), channel_id=1, replica_groups=mesh['dp'=4,'mp'=8] {'mp'}, use_global_device_ids=true, to_apply=%region_11.12 | all-reduce | flops 576 | bytes 4608 | tf_op jit(solution)/shard_map/psum | solution.py:49
  389.1 57.3 %reduce-scatter.31.cloned.1.call-done = bf16[128,288]{1,0:T(8,128)(2,1)} async-done(((bf16[1024,288]{1,0:T(8,128)(2,1)}), bf16[128,288]{1,0:T(8,128)(2,1)}) %reduce-scatter.31.cloned.1.call-update) | async-done | bytes 73744
  449.0 29.7 %all_gather.28 = bf16[288,1024]{1,0:T(8,128)(2,1)S(1)} all-gather(bf16[288,128]{1,0:T(8,128)(2,1)S(1)} %add_convert_fusion.1), channel_id=1, replica_groups=mesh['dp'=4,'mp'=8] {'mp'}, dimensions={1}, use_global_device_ids=true | all-gather | bytes 663552 | tf_op jit(solution)/shard_map/all_gather | solution.py:161
  480.9 25.6 %all-gather.7.cloned.1.call-done = bf16[288,4096]{1,0:T(8,128)(2,1)} async-done(((bf16[288,512]{1,0:T(8,128)(2,1)}), bf16[288,4096]{1,0:T(8,128)(2,1)}) %all-gather.7.cloned.1.call-update) | async-done | bytes 2359312 | tf_op jit(solution)/shard_map/all_gather | solution.py:172
  506.4 6.4 add_convert_fusion
  517.3 60.9 %reduce-scatter.33.cloned.1.call-done = bf16[128,288]{1,0:T(8,128)(2,1)} async-done(((bf16[1024,288]{1,0:T(8,128)(2,1)}), bf16[128,288]{1,0:T(8,128)(2,1)}) %reduce-scatter.33.cloned.1.call-update) | async-done | bytes 73744
  579.1 27.4 %all_gather.30 = bf16[288,1024]{1,0:T(8,128)(2,1)S(1)} all-gather(bf16[288,128]{1,0:T(8,128)(2,1)S(1)} %copy.191), channel_id=1, replica_groups=mesh['dp'=4,'mp'=8] {'mp'}, dimensions={1}, use_global_device_ids=true | all-gather | bytes 663552 | tf_op jit(solution)/shard_map/all_gather | solution.py:70
  608.2 18.4 %all-reduce.3 = (f32[288]{0:T(512)S(1)}, f32[288]{0:T(512)S(1)}) all-reduce(f32[288]{0:T(512)S(1)} %get-tuple-element.77, f32[288]{0:T(512)S(1)} %get-tuple-element.78), channel_id=1, replica_groups=mesh['dp'=4,'mp'=8] {'mp'}, use_global_device_ids=true, to_apply=%region_18.19 | all-reduce | flops 576 | bytes 4608 | tf_op jit(solution)/shard_map/psum | solution.py:80
  626.8 28.9 %all_gather.31 = bf16[288,1024]{1,0:T(8,128)(2,1)} all-gather(bf16[288,128]{1,0:T(8,128)(2,1)S(1)} %fusion.109), channel_id=1, replica_groups=mesh['dp'=4,'mp'=8] {'mp'}, dimensions={1}, use_global_device_ids=true | all-gather | bytes 663552 | tf_op jit(solution)/shard_map/all_gather | solution.py:86
  668.5 60.6 %reduce-scatter.35.cloned.1.call-done = bf16[128,288]{1,0:T(8,128)(2,1)} async-done(((bf16[1024,288]{1,0:T(8,128)(2,1)}), bf16[128,288]{1,0:T(8,128)(2,1)}) %reduce-scatter.35.cloned.1.call-update) | async-done | bytes 73744
  736.7 52.8 %all-gather.9.cloned.1.call-done = bf16[1152,1024]{1,0:T(8,128)(2,1)} async-done(((bf16[1152,128]{1,0:T(8,128)(2,1)}), bf16[1152,1024]{1,0:T(8,128)(2,1)}) %all-gather.9.cloned.1.call-update) | async-done | bytes 2359312 | tf_op jit(solution)/shard_map/all_gather | solution.py:70
  793.6 34.9 %all-reduce.2 = (f32[1152]{0:T(1024)}, f32[1152]{0:T(1024)}) all-reduce(f32[1152]{0:T(1024)} %get-tuple-element.71, f32[1152]{0:T(1024)} %get-tuple-element.72), channel_id=1, replica_groups=mesh['dp'=4,'mp'=8] {'mp'}, use_global_device_ids=true, to_apply=%region_23.24 | all-reduce | flops 2304 | bytes 18432 | tf_op jit(solution)/shard_map/psum | solution.py:80
  842.0 6.2 convolution_convert_fusion
  854.4 28.7 %all-gather.11.cloned.1.call-done = bf16[1152,1024]{1,0:T(8,128)(2,1)} async-done(((bf16[1152,128]{1,0:T(8,128)(2,1)}), bf16[1152,1024]{1,0:T(8,128)(2,1)}) %all-gather.11.cloned.1.call-update) | async-done | bytes 2359312 | tf_op jit(solution)/shard_map/all_gather | solution.py:86
  897.8 7.7 fusion.9
  928.5 25.8 %reduce-scatter.23.cloned.1.call-done = bf16[288,512]{1,0:T(8,128)(2,1)} async-done(((bf16[288,4096]{1,0:T(8,128)(2,1)}), bf16[288,512]{1,0:T(8,128)(2,1)}) %reduce-scatter.23.cloned.1.call-update) | async-done | bytes 294928 | tf_op jit(solution)/shard_map/reduce_scatter | solution.py:165
  963.9 62.5 %reduce-scatter.37.cloned.1.call-done = bf16[128,1152]{1,0:T(8,128)(2,1)} async-done(((bf16[1024,1152]{1,0:T(8,128)(2,1)}), bf16[128,1152]{1,0:T(8,128)(2,1)}) %reduce-scatter.37.cloned.1.call-update) | async-done | bytes 294928
  1028.4 199.1 %all-reduce.10.cloned.1.call-done = (bf16[1024,128]{0,1:T(8,128)(2,1)}, bf16[3,3,128,1024]{3,2,1,0:T(8,128)(2,1)}, bf16[128,1024]{1,0:T(8,128)(2,1)}, bf16[1024,...) async-done(((bf16[1024,128]{0,1:T(8,128)(2,1)}, ...) | async-done | bytes 11010064 | tf_op jit(solution)/shard_map/psum | solution.py:209
  (271 shorter events, 171.4 us)
Async XLA Ops:
  7.2 59.4 %all-gather.5.cloned.1.call-start = ((), (), s32[]{:S(2)}) async-start(), calls=%async_computation.8 | async-start | bytes 2654208 | tf_op jit(solution)/shard_map/all_gather | solution.py:36
  7.9 143.6 %reduce-scatter.25.cloned.1.call-start = ((), (), s32[]{:S(2)}) async-start(), calls=%async_computation.13 | async-start | bytes 2654208
  84.0 103.9 %copy-start.48 = (f32[128]{0:T(128)S(1)}, f32[128]{0:T(128)}, u32[]{:S(2)}) copy-start(f32[128]{0:T(128)} %param.19) | copy-start | bytes 1540
  84.0 103.9 %copy-start.57 = (bf16[128,1024]{1,0:T(8,128)(2,1)S(1)}, bf16[128,1024]{1,0:T(8,128)(2,1)}, u32[]{:S(2)}) copy-start(bf16[128,1024]{1,0:T(8,128)(2,1)} %param.18) | copy-start | bytes 786436
  84.0 103.9 %copy-start.60 = (f32[128]{0:T(128)S(1)}, f32[128]{0:T(128)}, u32[]{:S(2)}) copy-start(f32[128]{0:T(128)} %param.20) | copy-start | bytes 1540
  84.1 176.9 %reduce-scatter.27.cloned.1.call-start = ((), (), s32[]{:S(2)}) async-start(), calls=%async_computation.14 | async-start | bytes 2654208
  194.5 167.8 %reduce-scatter.29.cloned.1.call-start = ((), (), s32[]{:S(2)}) async-start(), calls=%async_computation.15 | async-start | bytes 884736
  302.4 144.0 %reduce-scatter.31.cloned.1.call-start = ((), (), s32[]{:S(2)}) async-start(), calls=%async_computation.16 | async-start | bytes 884736
  382.8 243.8 %copy-start.42 = (f32[288]{0:T(512)}, f32[288]{0:T(512)S(1)}, u32[]{:S(2)}) copy-start(f32[288]{0:T(512)S(1)} %get-tuple-element.108) | copy-start | bytes 3460
  382.8 243.8 %copy-start.44 = (f32[288]{0:T(512)}, f32[288]{0:T(512)S(1)}, u32[]{:S(2)}) copy-start(f32[288]{0:T(512)S(1)} %get-tuple-element.109) | copy-start | bytes 3460
  384.1 95.5 %copy-start.5 = (bf16[1024,512]{1,0:T(8,128)(2,1)S(1)}, bf16[1024,512]{1,0:T(8,128)(2,1)}, u32[]{:S(2)}) copy-start(bf16[1024,512]{1,0:T(8,128)(2,1)} %param.26) | copy-start | bytes 3145732
  386.4 120.0 %all-gather.7.cloned.1.call-start = ((), (), s32[]{:S(2)}) async-start(), calls=%async_computation.10 | async-start | bytes 2654208 | tf_op jit(solution)/shard_map/all_gather | solution.py:172
  387.3 125.6 %copy-start.40 = (f32[288]{0:T(512)}, f32[288]{0:T(512)S(1)}, u32[]{:S(2)}) copy-start(f32[288]{0:T(512)S(1)} %mul.273) | copy-start | bytes 3460
  389.1 189.0 %reduce-scatter.33.cloned.1.call-start = ((), (), s32[]{:S(2)}) async-start(), calls=%async_computation.17 | async-start | bytes 884736
  514.9 92.4 %copy-start.29 = (bf16[288,128]{1,0:T(8,128)(2,1)S(1)}, bf16[288,128]{1,0:T(8,128)(2,1)}, u32[]{:S(2)}) copy-start(bf16[288,128]{1,0:T(8,128)(2,1)} %copy-done.28) | copy-start | bytes 221188
  514.9 92.4 %copy-start.56 = (bf16[128,1024]{1,0:T(8,128)(2,1)S(1)}, bf16[128,1024]{1,0:T(8,128)(2,1)}, u32[]{:S(2)}) copy-start(bf16[128,1024]{1,0:T(8,128)(2,1)} %param.23) | copy-start | bytes 786436
  517.2 211.9 %reduce-scatter.35.cloned.1.call-start = ((), (), s32[]{:S(2)}) async-start(), calls=%async_computation.18 | async-start | bytes 884736
  666.2 123.4 %copy-start.7 = (bf16[1152,128]{1,0:T(8,128)(2,1)S(1)}, bf16[1152,128]{1,0:T(8,128)(2,1)}, u32[]{:S(2)}) copy-start(bf16[1152,128]{1,0:T(8,128)(2,1)} %copy-done.6) | copy-start | bytes 884740
  668.5 121.1 %all-gather.9.cloned.1.call-start = ((), (), s32[]{:S(2)}) async-start(), calls=%async_computation.11 | async-start | bytes 2654208 | tf_op jit(solution)/shard_map/all_gather | solution.py:70
  736.7 146.4 %all-gather.11.cloned.1.call-start = ((), (), s32[]{:S(2)}) async-start(), calls=%async_computation.12 | async-start | bytes 2654208 | tf_op jit(solution)/shard_map/all_gather | solution.py:86
  832.0 122.4 %reduce-scatter.23.cloned.1.call-start = ((), (), s32[]{:S(2)}) async-start(), calls=%async_computation.9 | async-start | bytes 2654208 | tf_op jit(solution)/shard_map/reduce_scatter | solution.py:165
  839.1 187.2 %reduce-scatter.37.cloned.1.call-start = ((), (), s32[]{:S(2)}) async-start(), calls=%async_computation.19 | async-start | bytes 2654208
  910.8 316.6 %all-reduce.10.cloned.1.call-start = ((), (), s32[]{:S(2)}) async-start(), calls=%async_computation.20 | async-start | bytes 22020096 | tf_op jit(solution)/shard_map/psum | solution.py:209
  928.5 99.0 %copy-start.3 = (f32[2,12,2,12,2,128]{5,4,3,2,1,0:T(2,128)S(1)}, f32[2,12,2,12,2,128]{5,4,3,2,1,0:T(2,128)}, u32[]{:S(2)}) copy-start(f32[2,12,2,12,2,128]{5,4,3,2,1,0:T(2,128)} %copy-done.2) | copy-start | bytes 1769476
  (53 other events, 806.0 us)
Sparse Core Ops, SparseCore 0:
  10.1 56.4 all-gather.4
  84.2 67.2 reduce-scatter.24
  194.6 66.2 reduce-scatter.26
  302.5 59.6 reduce-scatter.28
  386.5 59.8 reduce-scatter.30
  448.9 57.5 all-gather.6
  517.3 60.7 reduce-scatter.32
  668.6 60.5 reduce-scatter.34
  736.8 52.7 all-gather.8
  832.1 50.9 all-gather.10
  886.6 67.6 reduce-scatter.22
  958.3 68.0 reduce-scatter.36
  1030.6 196.7 all-reduce.9
where the time goes:
time: 1260 us; the launch traced here: 1250 us
  waiting for transfers between devices  826 us (66%)
  blocking collectives  227 us (18%)
  matrix products  78.4 us (6%)
  local copies, waits for them, and re-layouts  66.6 us (5%)
  other arithmetic  39.4 us (3%)
  between operations  15.8 us (1%)
    unnamed x20, waiting for transfers between devices  436 us
    psum x1, waiting for transfers between devices, body(): lax.psum(first_grads[0].astype(jnp.bfloat16), 'dp').astype(jnp.float32)  199 us
    all_gather x1, waiting for transfers between devices, block_forward(): full_in = lax.all_gather(low_in, 'mp', axis=1, tiled=True)  58.6 us
    psum x2, blocking collectives, block_forward(): lax.psum((jnp.sum(mixed_sum, axis=1), jnp.sum(mixed_sum * mixed_sum, axis...  54.2 us
    psum x2, blocking collectives, block_backward(): lax.psum((jnp.sum(scaled, axis=1), jnp.sum(scaled * normed, axis=1)), 'mp')  53.2 us
    all_gather x1, waiting for transfers between devices, block_backward(): lax.all_gather(grad_rows.astype(jnp.bfloat16), 'mp', axis=1, tiled=True)  52.8 us
    unnamed x143, local copies, waits for them, and re-layouts  40.8 us
    all_gather x1, blocking collectives, body(): flat_full = lax.all_gather(flat, 'mp', axis=1, tiled=True)  29.7 us
  transfers between devices with their start and end apart: 13, of which 13 were waited for; matrix products, arithmetic and copies ran while one was open for 6% of the time, Pallas kernels for 0%

commit v1 on v0

--- a/solution.py
+++ b/solution.py
@@ -1,6 +1,11 @@
+import functools
+
 import jax
 import jax.numpy as jnp
+import numpy as np
 from jax import lax
+from jax.experimental import pallas as pl
+from jax.experimental.pallas import tpu as pltpu
 from jax.sharding import PartitionSpec as P
 
 norm_eps = 1e-06
@@ -237,6 +242,929 @@
     )
 
 
+MESH = pl.DeviceIdType.MESH
+F32 = jnp.float32
+BF16 = jnp.bfloat16
+DMA = pltpu.SemaphoreType.DMA
+VMEM_LIMIT = 60 * 2**20
+ROW_PAD = 16
+
+
+def dot_nn(a, b):
+    return lax.dot_general(a, b, (((1,), (0,)), ((), ())), preferred_element_type=F32)
+
+
+def dot_nt(a, b):
+    return lax.dot_general(a, b, (((1,), (1,)), ((), ())), preferred_element_type=F32)
+
+
+def dot_tn(a, b):
+    return lax.dot_general(a, b, (((0,), (0,)), ((), ())), preferred_element_type=F32)
+
+
+def dot_full(a, b):
+    return lax.dot_general(
+        a,
+        b,
+        (((1,), (0,)), ((), ())),
+        precision=lax.Precision.HIGHEST,
+        preferred_element_type=F32,
+    )
+
+
+def sigmoid(values):
+    return 1.0 / (1.0 + jnp.exp(-values))
+
+
+def silu(values):
+    return values * sigmoid(values)
+
+
+def silu_slope(values):
+    gate = sigmoid(values)
+    return gate * (1.0 + values * (1.0 - gate))
+
+
+class Ring:
+    def __init__(self, size):
+        self.size = size
+        self.reach = size // 2
+        self.me = lax.axis_index("mp")
+        half = self.me // 2
+        self.spot = jnp.where(self.me % 2 == 0, half, size - 1 - half)
+        self.right = self.index(self.spot + 1)
+        self.left = self.index(self.spot - 1)
+
+    def wrap(self, spot):
+        return lax.rem(spot + 2 * self.size, self.size)
+
+    def index(self, spot):
+        spot = self.wrap(spot)
+        return jnp.where(spot < self.reach, 2 * spot, 2 * (self.size - 1 - spot) + 1)
+
+    def greet(self):
+        barrier = pltpu.get_barrier_semaphore()
+        for peer in (self.left, self.right):
+            pl.semaphore_signal(barrier, inc=1, device_id={"mp": peer}, device_id_type=MESH)
+        pl.semaphore_wait(barrier, 2)
+
+    def copy(self, side, src, dst, send, recv):
+        peer = self.right if side == 0 else self.left
+        return pltpu.make_async_remote_copy(
+            src_ref=src,
+            dst_ref=dst,
+            send_sem=send,
+            recv_sem=recv,
+            device_id={"mp": peer},
+            device_id_type=MESH,
+        )
+
+
+class Gather:
+    def __init__(self, ring, own, held, slot, halves, send, recv):
+        self.ring, self.own, self.held, self.slot = ring, own, held, slot
+        self.halves, self.send, self.recv, self.copies = halves, send, recv, {}
+
+    def _start(self, step):
+        ring = self.ring
+        for side in range(2):
+            away = step - 1
+            spot = ring.wrap(ring.spot - away if side == 0 else ring.spot + away)
+            dst = self.held.at[self.slot(spot)]
+            src = self.own if step == 1 else dst
+            if step == ring.reach:
+                src, dst = (ref.at[self.halves[side]] for ref in (src, dst))
+            copy = ring.copy(
+                side, src, dst, self.send.at[side, step - 1], self.recv.at[side, step - 1]
+            )
+            copy.start()
+            self.copies[side, step] = copy
+
+    def start(self):
+        self._start(1)
+
+    def arrive(self, step):
+        for side in range(2):
+            self.copies[side, step].wait_recv()
+
+    def forward(self, step):
+        self._start(step + 1)
+
+    def drain(self):
+        for copy in self.copies.values():
+            copy.wait_send()
+
+    def spots(self, step):
+        ring = self.ring
+        if step == ring.reach:
+            return [ring.wrap(ring.spot + step)]
+        return [ring.wrap(ring.spot - step), ring.wrap(ring.spot + step)]
+
+
+class Scatter:
+    def __init__(self, ring, term, out, terms, halves, send, recv):
+        self.ring, self.term, self.out, self.inbox = ring, term, out[0], out[1]
+        self.terms, self.halves, self.send, self.recv, self.copies = terms, halves, send, recv, {}
+
+    def _start(self, side, step):
+        src, dst = self.out.at[side, step - 1], self.inbox.at[side, step - 1]
+        if step == 1:
+            src, dst = (ref.at[self.halves[side]] for ref in (src, dst))
+        copy = self.ring.copy(
+            side, src, dst, self.send.at[side, step - 1], self.recv.at[side, step - 1]
+        )
+        copy.start()
+        self.copies[side, step] = copy
+
+    def start(self):
+        ring = self.ring
+        value = self.term(ring.wrap(ring.spot + ring.reach)).astype(BF16)
+        for side in range(2):
+            self.out[side, 0] = value
+            self._start(side, 1)
+
+    def prepare(self, step):
+        ring = self.ring
+        away = ring.reach + 1 - step
+        self.terms[0] = self.term(ring.wrap(ring.spot + away))
+        if away > 0:
+            self.terms[1] = self.term(ring.wrap(ring.spot - away))
+
+    def step(self, step):
+        for side in range(2):
+            self.copies[side, step - 1].wait_recv()
+            if step == 2:
+                mine, other = self.halves[side], self.halves[1 - side]
+                got = self.inbox[(side, 0) + mine].astype(F32)
+                self.out[(side, 1) + mine] = (self.terms[(side,) + mine] + got).astype(BF16)
+                self.out[(side, 1) + other] = self.terms[(side,) + other].astype(BF16)
+            else:
+                got = self.inbox[side, step - 2].astype(F32)
+                self.out[side, step - 1] = (self.terms[side] + got).astype(BF16)
+            self._start(side, step)
+
+    def finish(self):
+        reach = self.ring.reach
+        for side in range(2):
+            self.copies[side, reach].wait_recv()
+        return (
+            self.terms[0]
+            + self.inbox[0, reach - 1].astype(F32)
+            + self.inbox[1, reach - 1].astype(F32)
+        )
+
+    def drain(self):
+        for copy in self.copies.values():
+            copy.wait_send()
+
+    def run(self):
+        reach = self.ring.reach
+        self.start()
+        for step in range(2, reach + 1):
+            self.prepare(step)
+            self.step(step)
+        self.prepare(reach + 1)
+        return self.finish()
+
+
+def run_gather(gather, each=None):
+    reach = gather.ring.reach
+    gather.start()
+    for step in range(1, reach + 1):
+        gather.arrive(step)
+        if step < reach:
+            gather.forward(step)
+        if each is not None:
+            for spot in gather.spots(step):
+                each(spot)
+
+
+def row_halves(rows):
+    return ((pl.ds(0, rows // 2),), (pl.ds(rows // 2, rows // 2),))
+
+
+def column_halves(columns):
+    every = slice(None)
+    return (
+        (every, pl.ds(0, columns // 2)),
+        (every, pl.ds(columns // 2, columns // 2)),
+    )
+
+
+def pool_places(side):
+    small = side // 2
+    place = np.zeros((3 * ROW_PAD, 6 * side), np.float32)
+    for row in range(6):
+        for column in range(side):
+            place[(row // 2) * ROW_PAD + column // 2, row * side + column] = 0.25
+    assert small <= ROW_PAD
+    return place
+
+
+def token_places(grids, small):
+    place = np.zeros((grids * small * small, grids * small * ROW_PAD), np.float32)
+    for line in range(grids * small):
+        for column in range(small):
+            place[line * small + column, line * ROW_PAD + column] = 1.0
+    return place
+
+
+def norm_rows(mixed, gain, shift):
+    center = jnp.mean(mixed, axis=1, keepdims=True)
+    apart = mixed - center
+    inv_std = lax.rsqrt(jnp.mean(apart * apart, axis=1, keepdims=True) + norm_eps)
+    normed = apart * inv_std
+    return normed, inv_std, normed * gain + shift
+
+
+def wide_vector(held, row):
+    return jnp.concatenate([held[m, row : row + 1, :] for m in range(held.shape[0])], axis=1)
+
+
+def spread_taps(image, taps, grids, side, width):
+    chans = image.shape[-1]
+    rows = side * width
+
+    def one(g, carry):
+        for kh in range(3):
+            for kw in range(3):
+                piece = image[g, kh : kh + side, 7 + kw : 7 + kw + width, :]
+                at = (kh * 3 + kw) * chans
+                taps[pl.ds(pl.multiple_of(g * rows, 16), rows), at : at + chans] = (
+                    piece.reshape(rows, chans).astype(BF16)
+                )
+        return carry
+
+    lax.fori_loop(0, grids, one, 0)
+
+
+def collect_taps(image, product, grids, side, width):
+    chans = image.shape[-1]
+    rows = side * width
+
+    def one(g, carry):
+        image[g] = jnp.zeros(image.shape[1:], F32)
+        for kh in range(3):
+            for kw in range(3):
+                at = (kh * 3 + kw) * chans
+                piece = product[pl.ds(pl.multiple_of(g * rows, 16), rows), at : at + chans]
+                image[g, kh : kh + side, 7 + kw : 7 + kw + width, :] += piece.reshape(
+                    side, width, chans
+                )
+        return carry
+
+    lax.fori_loop(0, grids, one, 0)
+
+
+def first_forward(
+    size, grids, side,
+    x, reduce_w, mixer_w, expand_w, vectors, pool,
+    x_full, pre, taps, normed, inv_std, branch_sum, pooled, expand_full, vec_full,
+    image, out, terms, x_rows, send, recv,
+):
+    ring = Ring(size)
+    ring.greet()
+    rows, chans = x.shape
+    share = rows // size
+    x_full[ring.me] = x[...]
+    expand_full[ring.me] = expand_w[...]
+    vec_full[ring.me] = vectors[...]
+    gx = Gather(ring, x, x_full, ring.index, row_halves(rows), send.at[0], recv.at[0])
+    ge = Gather(ring, expand_w, expand_full, ring.index, row_halves(chans), send.at[1], recv.at[1])
+    gv = Gather(ring, vectors, vec_full, ring.index, row_halves(16), send.at[2], recv.at[2])
+
+    def add(spot):
+        m = ring.index(spot)
+        weight = reduce_w[pl.ds(pl.multiple_of(m * chans, chans), chans), :]
+        pre[...] += dot_nn(x_full[m], weight)
+
+    own = reduce_w[pl.ds(pl.multiple_of(ring.me * chans, chans), chans), :]
+    pre[...] = dot_nn(x[...], own)
+    image[...] = jnp.zeros(image.shape, F32)
+    run_gather(gx, add)
+    run_gather(ge)
+    run_gather(gv)
+    hidden = silu(pre[...])
+    image[:, 1 : 1 + side, 8 : 8 + side, :] = hidden.reshape(grids, side, side, chans)
+    spread_taps(image, taps, grids, side, side)
+
+    def term(spot):
+        return dot_nn(taps[pl.ds(pl.multiple_of(spot * share, 16), share), :], mixer_w[...])
+
+    total = size * chans
+    rs = Scatter(
+        ring, term, (out.at[0], out.at[1]), terms, column_halves(total), send.at[3], recv.at[3]
+    )
+    mixed = rs.run()
+    gain, shift = wide_vector(vec_full, 0), wide_vector(vec_full, 1)
+    value, inverse, affine = norm_rows(mixed, gain, shift)
+    normed[...] = value
+    inv_std[...] = jnp.broadcast_to(inverse, inv_std.shape)
+    branch = silu(affine).astype(BF16)
+    result = dot_nn(branch, expand_full[...].reshape(total, total))
+    mine = pl.ds(pl.multiple_of(ring.spot * share, 16), share)
+    for m in range(size):
+        x_rows[:, m * chans : (m + 1) * chans] = x_full[m, mine, :].astype(F32)
+    pooled[...] = dot_full(pool[...], x_rows[...] + result)
+    branch_sum[...] = (4.0 * dot_full(pool[...], branch.astype(F32))).astype(BF16)
+    for item in (gx, ge, gv, rs):
+        item.drain()
+
+
+def second_forward(
+    size, grids, small,
+    pooled, reduce_w, mixer_w, expand_w, vec_full, readout_in, readout_out, cotangent, live, places,
+    x_full, pre, taps, normed, inv_std, branch, expand_full, grad_rows, tokens, out_grad, in_grad,
+    image, own, flat_full, cot_full, lifted, act_live, grad_act, grad_lift, out, terms, tok_out, tok_terms, send, recv,
+):
+    ring = Ring(size)
+    ring.greet()
+    share, total = pooled.shape
+    chans = total // size
+    rows = size * share
+    part = readout_in.shape[1]
+    near = lambda spot: spot
+    own[0] = pooled[...].astype(BF16)
+    x_full[ring.spot] = own[0]
+    expand_full[ring.me] = expand_w[...]
+    cot_full[ring.me] = cotangent[...]
+    gx = Gather(ring, own.at[0], x_full, near, column_halves(total), send.at[0], recv.at[0])
+    ge = Gather(ring, expand_w, expand_full, ring.index, row_halves(chans), send.at[1], recv.at[1])
+    gc = Gather(
+        ring, cotangent, cot_full, ring.index, row_halves(cotangent.shape[0]), send.at[2], recv.at[2]
+    )
+    image[...] = jnp.zeros(image.shape, F32)
+    run_gather(gx)
+    run_gather(ge)
+    run_gather(gc)
+    pre[...] = dot_nn(x_full[...].reshape(rows, total), reduce_w[...])
+    hidden = silu(pre[...])
+    image[:, 1 : 1 + small, 8 : 8 + ROW_PAD, :] = hidden.reshape(grids, small, ROW_PAD, chans)
+    spread_taps(image, taps, grids, small, ROW_PAD)
+
+    def mix_term(spot):
+        return dot_nn(taps[pl.ds(pl.multiple_of(spot * share, 16), share), :], mixer_w[...])
+
+    halves = column_halves(total)
+    rs = Scatter(
+        ring, mix_term, (out.at[0], out.at[1]), terms, halves, send.at[3], recv.at[3]
+    )
+    mixed = rs.run()
+    gain, shift = wide_vector(vec_full, 2), wide_vector(vec_full, 3)
+    value, inverse, affine = norm_rows(mixed, gain, shift)
+    normed[...] = value
+    inv_std[...] = jnp.broadcast_to(inverse, inv_std.shape)
+    branch[...] = silu(affine).astype(BF16)
+    result = pooled[...] + dot_nn(branch[...], expand_full[...].reshape(total, total))
+    own[1] = result.astype(BF16)
+    flat_full[ring.spot] = own[1]
+    gf = Gather(ring, own.at[1], flat_full, near, halves, send.at[4], recv.at[4])
+    run_gather(gf)
+    flat = dot_nn(places[...], flat_full[...].reshape(rows, total)).astype(BF16)
+    lifted[...] = dot_nn(flat, readout_in[...])
+    cdf = 0.5 * (1.0 + lax.erf(lifted[...] * 0.7071067811865476))
+    activated = (lifted[...] * cdf).astype(BF16)
+    act_live[0] = activated
+    act_live[1] = (activated.astype(F32) * live[...]).astype(BF16)
+    grad_act[...] = jnp.zeros(grad_act.shape, F32)
+
+    def back(m, carry):
+        at = pl.ds(pl.multiple_of(m * part, 128), part)
+        grad_act[...] += dot_nt(cot_full[m], readout_out[:, at])
+        out_grad[:, at] = dot_tn(act_live[1], cot_full[m]).astype(BF16)
+        return carry
+
+    lax.fori_loop(0, size, back, 0)
+    slope = cdf + lifted[...] * jnp.exp(-0.5 * lifted[...] * lifted[...]) * 0.3989422804014327
+    lift = (grad_act[...] * live[...] * slope).astype(BF16)
+    in_grad[...] = dot_tn(flat, lift).astype(BF16)
+    grad_lift[...] = dot_tn(places[...], lift).astype(BF16)
+
+    def flat_term(spot):
+        return dot_nt(grad_lift[pl.ds(pl.multiple_of(spot * share, 16), share), :], readout_in[...])
+
+    rf = Scatter(
+        ring, flat_term, (out.at[2], out.at[3]), terms, halves, send.at[5], recv.at[5]
+    )
+    grad_rows[...] = rf.run()
+
+    def token_term(spot):
+        at = pl.ds(pl.multiple_of(ring.index(spot) * part, 128), part)
+        return dot_nn(act_live[0], readout_out[:, at])
+
+    rt = Scatter(
+        ring, token_term, (tok_out.at[0], tok_out.at[1]), tok_terms, column_halves(part), send.at[6], recv.at[6]
+    )
+    tokens[...] = (rt.run() * live[...]).astype(BF16)
+    for item in (gx, ge, gc, rs, gf, rf, rt):
+        item.drain()
+
+
+def norm_back(grad_branch, normed, inv_std, gain, shift):
+    affine = normed * gain + shift
+    grad_affine = grad_branch * silu_slope(affine)
+    gain_grad = jnp.sum(grad_affine * normed, axis=0, keepdims=True)
+    shift_grad = jnp.sum(grad_affine, axis=0, keepdims=True)
+    scaled = grad_affine * gain
+    mean_plain = jnp.mean(scaled, axis=1, keepdims=True)
+    mean_normed = jnp.mean(scaled * normed, axis=1, keepdims=True)
+    return inv_std * (scaled - mean_plain - normed * mean_normed), gain_grad, shift_grad
+
+
+def exchange_columns(ring, src, held, send, recv):
+    chans = held.shape[-1]
+    mine = pl.ds(pl.multiple_of(ring.me * chans, chans), chans)
+    held[ring.me] = src[:, mine]
+    copies = []
+    for away in range(1, ring.size):
+        peer = lax.rem(ring.me + away, ring.size)
+        copy = pltpu.make_async_remote_copy(
+            src_ref=src.at[:, pl.ds(pl.multiple_of(peer * chans, chans), chans)],
+            dst_ref=held.at[ring.me],
+            send_sem=send.at[away - 1],
+            recv_sem=recv.at[away - 1],
+            device_id={"mp": peer},
+            device_id_type=MESH,
+        )
+        copy.start()
+        copies.append(copy)
+    return copies
+
+
+def greet_all(ring):
+    barrier = pltpu.get_barrier_semaphore()
+    for away in range(1, ring.size):
+        peer = lax.rem(ring.me + away, ring.size)
+        pl.semaphore_signal(barrier, inc=1, device_id={"mp": peer}, device_id_type=MESH)
+    pl.semaphore_wait(barrier, ring.size - 1)
+
+
+def block_tail(ring, low, branch, low_full, branch_full, expand_grad, send, recv, asend, arecv):
+    total = low.shape[1]
+    copies = exchange_columns(ring, branch, branch_full, asend, arecv)
+    low_full[ring.spot] = low[...]
+    gl = Gather(ring, low, low_full, lambda spot: spot, column_halves(total), send, recv)
+    run_gather(gl)
+    for copy in copies:
+        copy.wait()
+    gl.drain()
+    expand_grad[...] = jnp.zeros(expand_grad.shape, BF16)
+    acc = None
+    for spot in range(ring.size):
+        m = 2 * spot if spot < ring.reach else 2 * (ring.size - 1 - spot) + 1
+        part = dot_tn(branch_full[m], low_full[spot])
+        acc = part if acc is None else acc + part
+    expand_grad[...] = acc.astype(BF16)
+
+
+def second_backward(
+    size, grids, small,
+    grad_rows, normed, inv_std, vec_full, branch, expand_full, taps, x_full, pre, mixer_w, reduce_w,
+    grad_in, mixer_grad, reduce_grad, expand_grad, vec_grad,
+    image, low, low_full, branch_full, mix_full, product, grad_pre, out, terms, send, recv, asend, arecv,
+):
+    ring = Ring(size)
+    greet_all(ring)
+    share, total = grad_rows.shape
+    rows = size * share
+    halves = column_halves(total)
+    gain, shift = wide_vector(vec_full, 2), wide_vector(vec_full, 3)
+    low[0] = grad_rows[...].astype(BF16)
+    grad_branch = dot_nt(low[0], expand_full[...].reshape(total, total))
+    mix, gain_grad, shift_grad = norm_back(
+        grad_branch, normed[...], inv_std[:, 0:1], gain, shift
+    )
+    vec_grad[0:1, :] = gain_grad
+    vec_grad[1:2, :] = shift_grad
+    low[1] = mix.astype(BF16)
+    mix_full[ring.spot] = low[1]
+    gm = Gather(ring, low.at[1], mix_full, lambda spot: spot, halves, send.at[0], recv.at[0])
+    run_gather(gm)
+    flat_mix = mix_full[...].reshape(rows, total)
+    product[...] = dot_nt(flat_mix, mixer_w[...])
+    collect_taps(image, product, grids, small, ROW_PAD)
+    grad_hidden = image[:, 1 : 1 + small, 8 : 8 + ROW_PAD, :].reshape(pre.shape)
+    grad_pre[...] = (grad_hidden * silu_slope(pre[...])).astype(BF16)
+
+    def term(spot):
+        return dot_nt(grad_pre[pl.ds(pl.multiple_of(spot * share, 16), share), :], reduce_w[...])
+
+    rs = Scatter(ring, term, (out.at[0], out.at[1]), terms, halves, send.at[1], recv.at[1])
+    grad_in[...] = rs.run() + grad_rows[...]
+    mixer_grad[...] = dot_tn(taps[...], flat_mix).astype(BF16)
+    reduce_grad[...] = dot_tn(x_full[...].reshape(rows, total), grad_pre[...]).astype(BF16)
+    block_tail(
+        ring, low.at[0], branch, low_full, branch_full, expand_grad, send.at[2], recv.at[2], asend, arecv
+    )
+    gm.drain()
+    rs.drain()
+
+
+def first_backward(
+    size, grids, side,
+    grad_pooled, spread, normed, inv_std, vec_full, branch_sum, expand_full, taps, x_full, pre, mixer_w, reduce_w,
+    patch_grads, mixer_grad, reduce_grad, expand_grad, vec_grad,
+    image, low, mix, low_full, branch_full, mix_full, product, grad_pre, grad_out, out, terms, send, recv, asend, arecv,
+):
+    ring = Ring(size)
+    greet_all(ring)
+    share, total = normed.shape
+    chans = total // size
+    rows = size * share
+    halves = column_halves(total)
+    gain, shift = wide_vector(vec_full, 0), wide_vector(vec_full, 1)
+    quarter = 0.25 * grad_pooled[...]
+    low[...] = quarter.astype(BF16)
+    grad_out[...] = dot_full(spread[...], quarter)
+    grad_small = dot_nt(low[...], expand_full[...].reshape(total, total))
+    grad_branch = dot_full(spread[...], grad_small)
+    value, gain_grad, shift_grad = norm_back(
+        grad_branch, normed[...], inv_std[:, 0:1], gain, shift
+    )
+    vec_grad[0:1, :] = gain_grad
+    vec_grad[1:2, :] = shift_grad
+    mix[...] = value.astype(BF16)
+    mix_full[ring.spot] = mix[...]
+    gm = Gather(ring, mix, mix_full, lambda spot: spot, halves, send.at[0], recv.at[0])
+    run_gather(gm)
+
+    def shares(q, carry):
+        product[pl.ds(pl.multiple_of(q * share, 16), share), :] = dot_nt(mix_full[q], mixer_w[...])
+        return carry
+
+    lax.fori_loop(0, size, shares, 0)
+    collect_taps(image, product, grids, side, side)
+    grad_hidden = image[:, 1 : 1 + side, 8 : 8 + side, :].reshape(pre.shape)
+    grad_pre[...] = (grad_hidden * silu_slope(pre[...])).astype(BF16)
+    mine = pl.ds(pl.multiple_of(ring.spot * share, 16), share)
+
+    def term(spot):
+        at = pl.multiple_of(ring.index(spot) * chans, chans)
+        return dot_nt(grad_pre[...], reduce_w[pl.ds(at, chans), :])
+
+    def term_and_rows(spot):
+        at = pl.ds(pl.multiple_of(ring.index(spot) * chans, chans), chans)
+        product[:, 0:chans] = term(spot)
+        product[mine, 0:chans] += grad_out[:, at]
+        return product[:, 0:chans]
+
+    rs = Scatter(
+        ring, term_and_rows, (out.at[0], out.at[1]), terms, row_halves(rows), send.at[1], recv.at[1]
+    )
+    patch_grads[...] = rs.run()
+
+    def weights(tap, carry):
+        at = pl.ds(pl.multiple_of(tap * chans, chans), chans)
+        mixer_grad[at, :] = dot_tn(
+            taps[:, at], mix_full[...].reshape(rows, total)
+        ).astype(BF16)
+        return carry
+
+    lax.fori_loop(0, 9, weights, 0)
+
+    def reduces(m, carry):
+        at = pl.ds(pl.multiple_of(m * chans, chans), chans)
+        reduce_grad[at, :] = dot_tn(x_full[m], grad_pre[...]).astype(BF16)
+        return carry
+
+    lax.fori_loop(0, size, reduces, 0)
+    block_tail(
+        ring, low, branch_sum, low_full, branch_full, expand_grad, send.at[2], recv.at[2], asend, arecv
+    )
+    gm.drain()
+    rs.drain()
+
+
+def sum_groups(count, *refs):
+    ins, outs = refs[:count], refs[count : 2 * count]
+    from_core, half_sum, from_far, final = (refs[(2 + k) * count : (3 + k) * count] for k in range(4))
+    send, recv = refs[6 * count :]
+    me = lax.axis_index("dp")
+    core = lax.rem(me, 2)
+    other = 1 - core
+    twin, far = me - core + other, lax.rem(me + 2, 4)
+    barrier = pltpu.get_barrier_semaphore()
+    for peer in (twin, far):
+        pl.semaphore_signal(barrier, inc=1, device_id={"dp": peer}, device_id_type=MESH)
+    pl.semaphore_wait(barrier, 2)
+
+    def go(step, k, src, dst, peer):
+        copy = pltpu.make_async_remote_copy(
+            src_ref=src,
+            dst_ref=dst,
+            send_sem=send.at[step, k],
+            recv_sem=recv.at[step, k],
+            device_id={"dp": peer},
+            device_id_type=MESH,
+        )
+        copy.start()
+        return copy
+
+    copies = {}
+
+    def half(k, which):
+        rows = ins[k].shape[0] // 2
+        return pl.ds(pl.multiple_of(which * rows, 16), rows)
+
+    for k in range(count):
+        copies[0, k] = go(0, k, ins[k].at[half(k, other)], from_core[k], twin)
+    for k in range(count):
+        copies[0, k].wait_recv()
+        mine = ins[k][half(k, core), :]
+        half_sum[k][...] = (mine.astype(F32) + from_core[k][...].astype(F32)).astype(BF16)
+        copies[1, k] = go(1, k, half_sum[k], from_far[k], far)
+    for k in range(count):
+        copies[1, k].wait_recv()
+        total = (half_sum[k][...].astype(F32) + from_far[k][...].astype(F32)).astype(BF16)
+        final[k][0] = total
+        copies[2, k] = go(2, k, final[k].at[0], final[k].at[1], twin)
+        outs[k][half(k, core), :] = total.astype(F32)
+    for k in range(count):
+        copies[2, k].wait_recv()
+        outs[k][half(k, other), :] = final[k][1].astype(F32)
+    for copy in copies.values():
+        copy.wait_send()
+
+
+def sum_vectors(size, vectors, result, held, sums, asend, arecv, bsend, brecv):
+    ring = Ring(size)
+    barrier = pltpu.get_barrier_semaphore()
+    me = lax.axis_index("dp")
+    groups = sums.shape[0]
+    for away in range(1, ring.size):
+        peer = lax.rem(ring.me + away, ring.size)
+        pl.semaphore_signal(barrier, inc=1, device_id={"mp": peer}, device_id_type=MESH)
+    for away in range(1, groups):
+        peer = lax.rem(me + away, groups)
+        pl.semaphore_signal(barrier, inc=1, device_id={"dp": peer}, device_id_type=MESH)
+    pl.semaphore_wait(barrier, ring.size - 1 + groups - 1)
+    for copy in exchange_columns(ring, vectors, held, asend, arecv):
+        copy.wait()
+    sums[me] = jnp.sum(held[...], axis=0)
+    copies = []
+    for away in range(1, groups):
+        copy = pltpu.make_async_remote_copy(
+            src_ref=sums.at[me],
+            dst_ref=sums.at[me],
+            send_sem=bsend.at[away - 1],
+            recv_sem=brecv.at[away - 1],
+            device_id={"dp": lax.rem(me + away, groups)},
+            device_id_type=MESH,
+        )
+        copy.start()
+        copies.append(copy)
+    for copy in copies:
+        copy.wait()
+    result[...] = jnp.sum(sums[...], axis=0)
+
+
+def kernel_call(kernel, name, number, outs, scratch, flops=0):
+    spec = pl.BlockSpec(memory_space=pltpu.VMEM)
+
+    def run(*args):
+        return pl.pallas_call(
+            kernel,
+            name=name,
+            out_shape=outs,
+            in_specs=[spec] * len(args),
+            out_specs=[spec] * len(outs),
+            scratch_shapes=scratch,
+            cost_estimate=pl.CostEstimate(flops=flops, bytes_accessed=0, transcendentals=0),
+            compiler_params=pltpu.CompilerParams(
+                collective_id=number, has_side_effects=True, vmem_limit_bytes=VMEM_LIMIT
+            ),
+        )(*args)
+
+    return run
+
+
+def fast_body(
+    size,
+    patches,
+    first_reduce,
+    first_mixer,
+    first_expand,
+    first_gain,
+    first_shift,
+    second_reduce,
+    second_mixer,
+    second_expand,
+    second_gain,
+    second_shift,
+    readout_in,
+    readout_out,
+    cotangent,
+    live_counts,
+):
+    S = jax.ShapeDtypeStruct
+    V = pltpu.VMEM
+    grids, side, _, chans = patches.shape
+    total = first_expand.shape[1]
+    rows = grids * side * side
+    share = rows // size
+    small = side // 2
+    few = 3 * ROW_PAD
+    few_rows = few * size
+    token_rows = grids * small * small
+    part = readout_in.shape[1]
+    wide = readout_out.shape[1]
+    reach = size // 2
+    pool = pool_places(side)
+    places = token_places(grids, small)
+    x = patches.reshape(rows, chans)
+    mixer_1 = first_mixer.reshape(9 * chans, total)
+    mixer_2 = second_mixer.reshape(9 * chans, total)
+    vectors = jnp.stack([first_gain, first_shift, second_gain, second_shift] * 4)
+    live_slots = (jnp.arange(grids) < live_counts[0]).astype(F32)
+    live = jnp.repeat(live_slots, small * small)[:, None]
+
+    outs = [
+        S((size, rows, chans), BF16),
+        S((rows, chans), F32),
+        S((rows, 9 * chans), BF16),
+        S((share, total), F32),
+        S((share, 128), F32),
+        S((few, total), BF16),
+        S((few, total), F32),
+        S((size, chans, total), BF16),
+        S((size, 16, chans), F32),
+    ]
+
+    def boxes(r, c):
+        return V((2, 2, reach, r, c), BF16)
+
+    scratch = [
+        V((grids, side + 2, side + 16, chans), F32),
+        boxes(share, total),
+        V((2, share, total), F32),
+        V((share, total), F32),
+        DMA((4, 2, reach)),
+        DMA((4, 2, reach)),
+    ]
+    x_full1, pre1, taps1, normed1, inv1, branch1, pooled, expand1, vec_full = kernel_call(
+        functools.partial(first_forward, size, grids, side), "first_forward", 1, outs, scratch
+    )(x, first_reduce, mixer_1, first_expand, vectors, pool)
+
+    outs = [
+        S((size, few, total), BF16),
+        S((few_rows, chans), F32),
+        S((few_rows, 9 * chans), BF16),
+        S((few, total), F32),
+        S((few, 128), F32),
+        S((few, total), BF16),
+        S((size, chans, total), BF16),
+        S((few, total), F32),
+        S((token_rows, part), BF16),
+        S((part, wide), BF16),
+        S((total, part), BF16),
+    ]
+    scratch = [
+        V((grids, small + 2, ROW_PAD + 16, chans), F32),
+        V((2, few, total), BF16),
+        V((size, few, total), BF16),
+        V((size, token_rows, part), BF16),
+        V((token_rows, part), F32),
+        V((2, token_rows, part), BF16),
+        V((token_rows, part), F32),
+        V((few_rows, part), BF16),
+        V((4, 2, reach, few, total), BF16),
+        V((2, few, total), F32),
+        boxes(token_rows, part),
+        V((2, token_rows, part), F32),
+        DMA((7, 2, reach)),
+        DMA((7, 2, reach)),
+    ]
+    (
+        x_full2, pre2, taps2, normed2, inv2, branch2, expand2, grad_rows, tokens, out_grad, in_grad,
+    ) = kernel_call(
+        functools.partial(second_forward, size, grids, small), "second_forward", 2, outs, scratch
+    )(
+        pooled, second_reduce, mixer_2, second_expand, vec_full, readout_in, readout_out, cotangent,
+        live, places.astype(BF16),
+    )
+
+    outs = [
+        S((few, total), F32),
+        S((9 * chans, total), BF16),
+        S((total, chans), BF16),
+        S((chans, total), BF16),
+        S((2, total), F32),
+    ]
+    scratch = [
+        V((grids, small + 2, ROW_PAD + 16, chans), F32),
+        V((2, few, total), BF16),
+        V((size, few, total), BF16),
+        V((size, few, chans), BF16),
+        V((size, few, total), BF16),
+        V((few_rows, 9 * chans), F32),
+        V((few_rows, chans), BF16),
+        boxes(few, total),
+        V((2, few, total), F32),
+        DMA((3, 2, reach)),
+        DMA((3, 2, reach)),
+        DMA((size - 1,)),
+        DMA((size - 1,)),
+    ]
+    grad_pooled, mixer_grad2, reduce_grad2, expand_grad2, vec_grad2 = kernel_call(
+        functools.partial(second_backward, size, grids, small), "second_backward", 3, outs, scratch
+    )(
+        grad_rows, normed2, inv2, vec_full, branch2, expand2, taps2, x_full2, pre2, mixer_2,
+        second_reduce,
+    )
+
+    outs = [
+        S((rows, chans), F32),
+        S((9 * chans, total), BF16),
+        S((total, chans), BF16),
+        S((chans, total), BF16),
+        S((2, total), F32),
+    ]
+    scratch = [
+        V((grids, side + 2, side + 16, chans), F32),
+        V((few, total), BF16),
+        V((share, total), BF16),
+        V((size, few, total), BF16),
+        V((size, few, chans), BF16),
+        V((size, share, total), BF16),
+        V((rows, 9 * chans), F32),
+        V((rows, chans), BF16),
+        V((share, total), F32),
+        boxes(rows, chans),
+        V((2, rows, chans), F32),
+        DMA((3, 2, reach)),
+        DMA((3, 2, reach)),
+        DMA((size - 1,)),
+        DMA((size - 1,)),
+    ]
+    patch_grads, mixer_grad1, reduce_grad1, expand_grad1, vec_grad1 = kernel_call(
+        functools.partial(first_backward, size, grids, side), "first_backward", 4, outs, scratch
+    )(
+        grad_pooled, np.ascontiguousarray(4.0 * pool.T), normed1, inv1, vec_full, branch1, expand1, taps1,
+        x_full1, pre1, mixer_1, first_reduce,
+    )
+
+    def group_sum(number, name, grads):
+        count = len(grads)
+        sums = [S(g.shape, F32) for g in grads]
+        halves = [(g.shape[0] // 2, g.shape[1]) for g in grads]
+        scratch = [V(h, BF16) for h in halves * 3] + [V((2,) + h, BF16) for h in halves]
+        scratch += [DMA((3, count)), DMA((3, count))]
+        return kernel_call(functools.partial(sum_groups, count), name, number, sums, scratch)(*grads)
+
+    out_sum, in_sum = group_sum(5, "sum_readout", [out_grad, in_grad])
+    sums = group_sum(
+        6,
+        "sum_blocks",
+        [mixer_grad2, reduce_grad2, expand_grad2, mixer_grad1, reduce_grad1, expand_grad1],
+    )
+    mixer2_sum, reduce2_sum, expand2_sum, mixer1_sum, reduce1_sum, expand1_sum = sums
+    groups = 4
+    vec_sum = kernel_call(
+        functools.partial(sum_vectors, size),
+        "sum_vectors",
+        7,
+        [S((8, chans), F32)],
+        [
+            V((size, 8, chans), F32),
+            V((groups, 8, chans), F32),
+            DMA((size - 1,)),
+            DMA((size - 1,)),
+            DMA((groups - 1,)),
+            DMA((groups - 1,)),
+        ],
+    )(jnp.concatenate([vec_grad1, vec_grad2] * 2))[0]
+    return (
+        tokens,
+        patch_grads.reshape(patches.shape),
+        reduce1_sum,
+        mixer1_sum.reshape(first_mixer.shape),
+        expand1_sum,
+        vec_sum[0],
+        vec_sum[1],
+        reduce2_sum,
+        mixer2_sum.reshape(second_mixer.shape),
+        expand2_sum,
+        vec_sum[2],
+        vec_sum[3],
+        in_sum,
+        out_sum,
+    )
+
+
+def fits(mesh, patches, first_reduce, readout_in):
+    size, groups = mesh.shape["mp"], mesh.shape["dp"]
+    grids, side, _, chans = patches.shape
+    return (
+        groups == 4
+        and size % 2 == 0
+        and chans % 128 == 0
+        and readout_in.shape[1] % 128 == 0
+        and grids * side == 6 * size
+        and side % 8 == 0
+        and side // 2 <= ROW_PAD
+    )
+
+
 def solution(mesh):
     in_specs = (
         P("dp", None, None, "mp"),
@@ -271,4 +1199,10 @@
         P(None, "mp"),
         P("mp", None),
     )
-    return jax.shard_map(body, mesh=mesh, in_specs=in_specs, out_specs=out_specs, check_vma=False)
+
+    def local(*args):
+        if fits(mesh, args[0], args[1], args[11]):
+            return fast_body(mesh.shape["mp"], *args)
+        return body(*args)
+
+    return jax.shard_map(local, mesh=mesh, in_specs=in_specs, out_specs=out_specs, check_vma=False)

time: 1260 us -> 599 us (0.48)
  waiting for transfers between devices: 826 us -> 0 us
  Pallas kernels: 0 us -> 571 us
  blocking collectives: 227 us -> 0 us
  matrix products: 78.4 us -> 0 us
  local copies, waits for them, and re-layouts: 66.6 us -> 24.8 us
  other arithmetic: 39.4 us -> 1.41 us
  between operations: 15.8 us -> 1.43 us
    pallas_call x0 -> x7, Pallas kernels: none -> 571 us  [run(): pl.pallas_call(kernel, name=name, out_shape=outs, in_specs=[spec] * len(a...]
    unnamed x20 -> x0, waiting for transfers between devices: 436 us -> none
    psum x1 -> x0, waiting for transfers between devices: 199 us -> none  [body(): lax.psum(first_grads[0].astype(jnp.bfloat16), 'dp').astype(jnp.float32)]
    all_gather x4 -> x0, waiting for transfers between devices: 166 us -> none  [the longest x1 58.6 us: block_forward(): full_in = lax.all_gather(low_in, 'mp', axis=1, tiled=True)]
    all_gather x4 -> x0, blocking collectives: 114 us -> none  [the longest x1 29.7 us: body(): flat_full = lax.all_gather(flat, 'mp', axis=1, tiled=True)]
    psum x5 -> x0, blocking collectives: 113 us -> none  [the longest x2 54.2 us: block_forward(): lax.psum((jnp.sum(mixed_sum, axis=1), jnp.sum(mixed_sum * mixed_sum, axis...]
    dot_general x36 -> x0, matrix products: 57.2 us -> none  [the longest x18 12.1 us: block_backward(): jnp.einsum('nhwi,nhwo->io', padded[:, offset_h:offset_h + grid_height, of...]
    convert_element_type x22 -> x1, other arithmetic: 28.5 us -> 0.01 us  [fast_body(): live_slots = (jnp.arange(grids) < live_counts[0]).astype(F32)]
  transfers between devices with their start and end apart: 13 -> 0, of which waited for: 13 -> 0; matrix products, arithmetic and copies ran while one was open for 6% -> 0% of each run, Pallas kernels for 0% -> 0%
where the time goes in v1:
time: 599 us; the launch traced here: 598 us
  Pallas kernels  571 us (95%)
  local copies, waits for them, and re-layouts  24.8 us (4%)
    pallas_call x7, Pallas kernels, run(): pl.pallas_call(kernel, name=name, out_shape=outs, in_specs=[spec] * len(a...  571 us
    unnamed x34, local copies, waits for them, and re-layouts  19.8 us

profile of v1, /device:TPU:0, one launch (start us, length us, event | category | flops | bytes accessed | tf_op | source)
XLA Modules:
  0.0 598.2 jit_solution(15805923433542500643)
XLA Ops:
  1.3 0.1 broadcast_in_dim.3
  1.4 2.7 stack.14.vectors
  4.1 0.9 broadcast_in_dim_reshape.4.live
  5.0 103.0 %first_forward.1 = (bf16[8,1152,128]{2,1,0:T(8,128)(2,1)}, f32[1152,128]{1,0:T(8,128)}, bf16[1152,1152]{1,0:T(8,128)(2,1)}, f32[144,1024]{1,0:T(8,128)}, f32[144...) custom-call(bf16[1152,128]{1,0:T(8,128)(2,1)} %bitcast.31, ...), custom_call_target="tpu_custom_call" | custom-call | tf_op jit(solution)/shard_map/first_forward/pallas_call | solution.py:925
  108.0 158.4 %second_forward.1 = (bf16[8,48,1024]{2,1,0:T(8,128)(2,1)}, f32[384,128]{1,0:T(8,128)}, bf16[384,1152]{1,0:T(8,128)(2,1)}, f32[48,1024]{1,0:T(8,128)}, f32[48,128...) custom-call(f32[48,1024]{1,0:T(8,128)} %get-tuple-element.52.pooled,, ...), custom_call_target="tpu_custom_call" | custom-call | tf_op jit(solution)/shard_map/second_forward/pallas_call | solution.py:925
  266.4 61.3 %second_backward.1 = (f32[48,1024]{1,0:T(8,128)}, bf16[1152,1024]{1,0:T(8,128)(2,1)}, bf16[1024,128]{1,0:T(8,128)(2,1)}, bf16[128,1024]{1,0:T(8,128)(2,1)}, f32[2,1024]{1,0:T(2,128)}) custom-call(f32[48,1024]{1,0:T(8,128)} %get-tuple-element.55.grad_rows, f32[48,1024]{1,0:T(8,128)} %get-tuple-element.56.normed, f32[48,128]{1,0:T(8,128)} %get-tuple-element.57.inv_std, ...), custom_call_target="tpu_custom_call" | custom-call | tf_op jit(solution)/shard_map/second_backward/pallas_call | solution.py:925
  327.7 88.5 %first_backward.1 = (f32[1152,128]{1,0:T(8,128)}, bf16[1152,1024]{1,0:T(8,128)(2,1)}, bf16[1024,128]{1,0:T(8,128)(2,1)}, bf16[128,1024]{1,0:T(8,128)(2,1)}, f32[2,1024]{1,0:T(2,128)}) custom-call(f32[48,1024]{1,0:T(8,128)} %get-tuple-element.63.grad_pooled, f32[144,48]{1,0:T(8,128)} %constant.8.clone.spread, f32[144,1024]{1,0:T(8,128)} %get-tuple-element.64.normed, ...), custom_call_target="tpu_custom_call" | custom-call | tf_op jit(solution)/shard_map/first_backward/pallas_call | solution.py:925
  416.2 1.4 pad_maximum_fusion.vectors
  417.6 11.3 %sum_vectors.1 = f32[8,128]{1,0:T(8,128)} custom-call(f32[8,1024]{1,0:T(8,128)} %pad_maximum_fusion.vectors), custom_call_target="tpu_custom_call" | custom-call | tf_op jit(solution)/shard_map/sum_vectors/pallas_call | solution.py:925
  428.9 1.4 slice_bitcast_fusion
  430.3 76.0 %sum_blocks.1 = (f32[1152,1024]{1,0:T(8,128)}, f32[1024,128]{1,0:T(8,128)}, f32[128,1024]{1,0:T(8,128)}, f32[1152,1024]{1,0:T(8,128)}, f32[1024,128]{1,0:T(8,128)}, /*index=5*/f32[128,1024]{1,0:T(8,128)}) custom-call(bf16[1152,1024]{1,0:T(8,128)(2,1)} %get-tuple-element.72.refs_0_, bf16[1024,128]{1,0:T(8,128)(2,1)} %get-tuple-element.73.refs_1_, ...), custom_call_target="tpu_custom_call" | custom-call | tf_op jit(solution)/shard_map/sum_blocks/pallas_call | solution.py:925
  506.3 72.0 %sum_readout.1 = (f32[512,4096]{1,0:T(8,128)}, f32[1024,512]{1,0:T(8,128)}) custom-call(bf16[512,4096]{1,0:T(8,128)(2,1)} %get-tuple-element.86.refs_0_, bf16[1024,512]{1,0:T(8,128)(2,1)} %get-tuple-element.87.refs_1_), custom_call_target="tpu_custom_call" | custom-call | tf_op jit(solution)/shard_map/sum_readout/pallas_call | solution.py:925
  578.4 0.7 copy.44
  579.1 0.8 copy.45
  579.9 0.8 copy.46
  580.7 6.1 %copy.47 = f32[3,3,128,1024]{3,2,1,0:T(8,128)} copy(f32[3,3,128,1024]{3,2,1,0:T(8,128)} %bitcast.29) | data formatting | bytes 9437184
  586.8 0.8 copy.48
  587.6 0.8 copy.49
  588.5 2.4 copy.50
  590.9 0.8 copy.51
  591.7 0.8 copy-done
  592.5 1.3 copy.52
  593.8 0.9 slice-done.1
  594.8 3.4 copy.53
  (25 shorter events, 0.0 us)
Async XLA Ops:
  327.7 88.5 %copy-start.7 = (f32[2,1024]{1,0:T(2,128)S(1)}, f32[2,1024]{1,0:T(2,128)}, u32[]{:S(2)}) copy-start(f32[2,1024]{1,0:T(2,128)} %get-tuple-element.82) | copy-start | bytes 24580
  506.3 72.1 %copy-start.6 = (bf16[288,512]{1,0:T(8,128)(2,1)S(1)}, bf16[288,512]{1,0:T(8,128)(2,1)}, u32[]{:S(2)}) copy-start(bf16[288,512]{1,0:T(8,128)(2,1)} %get-tuple-element.108) | copy-start | bytes 884740
  506.3 72.8 %copy-start.1 = (f32[1152,128]{1,0:T(8,128)S(1)}, f32[1152,128]{1,0:T(8,128)}, u32[]{:S(2)}) copy-start(f32[1152,128]{1,0:T(8,128)} %get-tuple-element.71) | copy-start | bytes 1769476
  506.3 73.6 %copy-start.5 = (f32[1024,128]{1,0:T(8,128)S(1)}, f32[1024,128]{1,0:T(8,128)}, u32[]{:S(2)}) copy-start(f32[1024,128]{1,0:T(8,128)} %get-tuple-element.110) | copy-start | bytes 1572868
  579.9 8.5 %slice-start.2 = ((s8[4718592]{0:T(1024)(128)(4,1)}), s8[4194304]{0:T(1024)(128)(4,1)S(1)}, s32[]{:S(2)}) async-start(s8[4718592]{0:T(1024)(128)(4,1)} %bitcast.26), calls=%async_computation.2 | async-start | bytes 8388608
  580.7 6.1 %copy-start.4 = (f32[128,1024]{1,0:T(8,128)S(1)}, f32[128,1024]{1,0:T(8,128)}, u32[]{:S(2)}) copy-start(f32[128,1024]{1,0:T(8,128)} %get-tuple-element.112) | copy-start | bytes 1572868
  580.7 6.9 %copy-start.3 = (f32[1024,128]{1,0:T(8,128)S(1)}, f32[1024,128]{1,0:T(8,128)}, u32[]{:S(2)}) copy-start(f32[1024,128]{1,0:T(8,128)} %get-tuple-element.115) | copy-start | bytes 1572868
  580.7 7.7 %slice-start.3 = ((s8[4718592]{0:T(1024)(128)(4,1)}), s8[524288]{0:T(1024)(128)(4,1)S(1)}, s32[]{:S(2)}) async-start(s8[4718592]{0:T(1024)(128)(4,1)} %bitcast.26), calls=%async_computation.3 | async-start | bytes 1048576
  587.6 3.2 copy-start.2
  587.6 6.2 %slice-start = ((s8[8388608]{0:T(1024)(128)(4,1)}), s8[4194304]{0:T(1024)(128)(4,1)S(1)}, s32[]{:S(2)}) async-start(s8[8388608]{0:T(1024)(128)(4,1)} %bitcast.24), calls=%async_computation | async-start | bytes 8388608
  588.4 4.1 copy-start
  588.4 6.3 %slice-start.1 = ((s8[8388608]{0:T(1024)(128)(4,1)}), s8[4194304]{0:T(1024)(128)(4,1)S(1)}, s32[]{:S(2)}) async-start(s8[8388608]{0:T(1024)(128)(4,1)} %bitcast.24), calls=%async_computation.1 | async-start | bytes 8388608
